TPU v7x, 128 devices: a whole 4x4x4 slice. The times are simulated.
128 devices in a mesh: row: 8 (over y_hi, z), col: 16 (over x, y_lo, core).
Axes of the slice: x: 4, y: 4 (y_hi: 2, y_lo: 2; y = y_hi * 2 + y_lo), z: 4, core: 2. Of those that a mesh axis runs over, the one named last changes fastest.
Arguments:
- tokens: bfloat16 [6144, 8192], P('row', 'col'), may hold values from -6 to 6
- gate_weight: bfloat16 [8192, 14336], P('row', 'col'), may hold values from -0.0625 to 0.0625
- up_weight: bfloat16 [8192, 14336], P('row', 'col'), may hold values from -0.0625 to 0.0625
Outputs:
- hidden: bfloat16 [6144, 14336], P('row', 'col')
All inputs are finite; a program needn't handle non-finite values.
Results may differ from a plain program's by a relative error of at most 0.0023.
Values may be sent and summed in bfloat16 or wider, within the bound.
A program may use at most 192 MiB of HBM per device.

v0:
```python
import jax
import jax.numpy as jnp
from jax import lax
from jax.sharding import PartitionSpec as P


def on_device(tokens, gate_weight, up_weight):
    features = lax.all_gather(tokens, "col", axis=1, tiled=True)
    first = jnp.dot(
        features,
        lax.all_gather(gate_weight, "row", axis=0, tiled=True),
        preferred_element_type=jnp.float32,
    )
    second = jnp.dot(
        features,
        lax.all_gather(up_weight, "row", axis=0, tiled=True),
        preferred_element_type=jnp.float32,
    )
    return (jax.nn.silu(first) * second).astype(jnp.bfloat16)


def solution(mesh):
    placed = (P("row", "col"), P("row", "col"), P("row", "col"))
    return jax.shard_map(
        on_device, mesh=mesh, in_specs=placed, out_specs=P("row", "col"), check_vma=False
    )
```

profile of v0, /device:TPU:0, one launch (start us, length us, event | category | flops | bytes accessed | tf_op | source)
XLA Modules:
  0.0 440.7 jit_solution(12636794565006994086)
XLA Ops:
  6.5 0.0 all-gather.4.cloned.1.call-start
  6.5 0.7 all-gather.4.cloned.1.call-update
  7.3 0.0 all-gather.6.cloned.1.call-start
  7.3 0.7 all-gather.6.cloned.1.call-update
  8.0 0.0 all-gather.8.cloned.1.call-start
  8.1 0.7 all-gather.8.cloned.1.call-update
  8.7 74.6 %all-gather.4.cloned.1.call-done = bf16[768,8192]{1,0:T(8,128)(2,1)} async-done(((bf16[768,512]{1,0:T(8,128)(2,1)}), bf16[768,8192]{1,0:T(8,128)(2,1)}) %all-gather.4.cloned.1.call-update) | async-done | bytes 12582928 | tf_op jit(solution)/shard_map/all_gather | solution.py:8
  83.4 167.2 %all-gather.6.cloned.1.call-done = bf16[8192,896]{1,0:T(8,128)(2,1)} async-done(((bf16[1024,896]{1,0:T(8,128)(2,1)}), bf16[8192,896]{1,0:T(8,128)(2,1)}) %all-gather.6.cloned.1.call-update) | async-done | bytes 14680080 | tf_op jit(solution)/shard_map/all_gather | solution.py:11
  250.6 17.8 %fusion = f32[768,896]{1,0:T(8,128)S(1)} fusion(bf16[768,8192]{1,0:T(8,128)(2,1)} %all-gather.4.cloned.1.call-done, bf16[8192,896]{1,0:T(8,128)(2,1)} %all-gather.6.cloned.1.call-done), kind=kOutput, calls=%fused_computation.1 | convolution fusion | flops 11274289152 | bytes 30015488 | tf_op jit(solution)/shard_map/dot_general | solution.py:9
  268.3 146.3 %all-gather.8.cloned.1.call-done = bf16[8192,896]{1,0:T(8,128)(2,1)} async-done(((bf16[1024,896]{1,0:T(8,128)(2,1)}), bf16[8192,896]{1,0:T(8,128)(2,1)}) %all-gather.8.cloned.1.call-update) | async-done | bytes 14680080 | tf_op jit(solution)/shard_map/all_gather | solution.py:16
  414.7 19.4 %multiply_convert_fusion = bf16[768,896]{1,0:T(8,128)(2,1)} fusion(f32[768,896]{1,0:T(8,128)S(1)} %fusion, bf16[768,8192]{1,0:T(8,128)(2,1)} %all-gather.4.cloned.1.call-done, bf16[8192,896]{1,0:T(8,128)(2,1)} %all-gather.8.cloned.1.call-done), kind=kOutput, calls=%fused_computation | convolution fusion | flops 11278417920 | bytes 31391744 | tf_op jit(solution)/shard_map/dot_general | solution.py:14
Async XLA Ops:
  6.5 76.8 %all-gather.4.cloned.1.call-start = ((), (), s32[]{:S(2)}) async-start(), calls=%async_computation | async-start | bytes 13369344 | tf_op jit(solution)/shard_map/all_gather | solution.py:8
  7.3 243.3 %all-gather.6.cloned.1.call-start = ((), (), s32[]{:S(2)}) async-start(), calls=%async_computation.1 | async-start | bytes 16515072 | tf_op jit(solution)/shard_map/all_gather | solution.py:11
  8.0 406.7 %all-gather.8.cloned.1.call-start = ((), (), s32[]{:S(2)}) async-start(), calls=%async_computation.2 | async-start | bytes 16515072 | tf_op jit(solution)/shard_map/all_gather | solution.py:16
Sparse Core Ops, SparseCore 0:
  9.0 74.2 all-gather.3
  85.7 164.8 all-gather.5
  252.9 161.7 all-gather.7
where the time goes:
time: 441 us
  waiting for transfers between devices  390 us (88%)
  matrix products  37.2 us (8%)
  between operations  13.1 us (3%)
    all_gather x1, waiting for transfers between devices, on_device(): lax.all_gather(gate_weight, 'row', axis=0, tiled=True)  167 us
    all_gather x1, waiting for transfers between devices, on_device(): lax.all_gather(up_weight, 'row', axis=0, tiled=True)  146 us
    all_gather x1, waiting for transfers between devices, on_device(): features = lax.all_gather(tokens, 'col', axis=1, tiled=True)  74.6 us
    dot_general x1, matrix products, on_device(): jnp.dot(features, lax.all_gather(up_weight, 'row', axis=0, tiled=True), p...  19.4 us
    dot_general x1, matrix products, on_device(): jnp.dot(features, lax.all_gather(gate_weight, 'row', axis=0, tiled=True),...  17.8 us
  transfers between devices with their start and end apart: 3, of which 3 were waited for; matrix products, arithmetic and copies ran while one was open for 4% of the time, Pallas kernels for 0%

commit v1 on v0

v1 whole, which is shorter than its diff:
```python
import functools

import jax
import jax.numpy as jnp
from jax import lax
from jax.experimental import pallas as pl
from jax.experimental.pallas import tpu as pltpu
from jax.sharding import PartitionSpec as P

MESH = pl.DeviceIdType.MESH
LANES = 128
PIECES = 3


def encode(v):
    w = v * 2.0**14
    w2 = w * w
    return (w2 * w2 * w).astype(jnp.bfloat16)


def decode(u):
    u = u.astype(jnp.float32)
    r = jnp.exp2(jnp.log2(jnp.abs(u)) * 0.2 - 14.0)
    return jnp.where(u < 0, -r, r)


def kernel(
    tok, gate, up, out,
    wb, tb, send, got, acc,
    w_in, w_out, w_local, t_in, t_sib, y_out, x_out, s_out, o_in, o_out,
):
    rows, half = tok.shape
    depth, units = gate.shape
    chunks = units // LANES
    piece = rows // PIECES
    row, col = lax.axis_index("row"), lax.axis_index("col")
    yh, z = row // 4, row % 4
    x, yl, core = col // 4, (col // 2) % 2, col % 2
    b = x % 2
    source = (x // 2) == yh
    y = yh * 2 + yl

    def at(x=x, y=y, z=z, core=core):
        return ((y // 2) * 4 + z, x * 4 + (y % 2) * 2 + core)

    z_next, z_prev = (z + 1) % 4, (z + 3) % 4
    x_next, x_prev = (x + 1) % 4, (x + 3) % 4
    right, left = at(z=z_next), at(z=z_prev)
    partner = at(y=(y + 2) % 4)
    flip = at(y=yh * 2 + 1 - yl)
    cross = at(y=(1 - yh) * 2 + 1 - yl)
    sibling = at(core=1 - core)
    pair = at(x=jnp.where(b == 0, x_next, x_prev))
    outer = at(x=jnp.where(b == 0, x_prev, x_next))

    def remote(src, dst, ssem, rsem, to):
        return pltpu.make_async_remote_copy(
            src_ref=src, dst_ref=dst, send_sem=ssem, recv_sem=rsem, device_id=to, device_id_type=MESH
        )

    def landed(ref, sem):
        pltpu.make_async_copy(ref, ref, sem).wait()

    def slot(n, s, lo=0, size=depth):
        return wb.at[n, pl.ds(pl.multiple_of(s * depth + lo, size), size), :]

    def pack(n):
        mine = pl.ds(pl.multiple_of(z * depth, depth), depth)
        lane = pl.ds(pl.multiple_of(n * LANES, LANES), LANES)
        return (
            pltpu.make_async_copy(gate.at[:, lane], wb.at[n, mine, pl.ds(0, LANES)], w_local.at[n, 0]),
            pltpu.make_async_copy(up.at[:, lane], wb.at[n, mine, pl.ds(LANES, LANES)], w_local.at[n, 1]),
        )

    def own_weights(n):
        mine = slot(n, z)
        return (
            remote(mine, mine, w_out.at[n, 0], w_in.at[n, 0], right),
            remote(mine, mine, w_out.at[n, 1], w_in.at[n, 1], left),
        )

    def relayed_weights(n):
        top = slot(n, z_prev, 0, depth // 2)
        low = slot(n, z_next, depth // 2, depth // 2)
        return (
            remote(top, top, w_out.at[n, 2], w_in.at[n, 2], right),
            remote(low, low, w_out.at[n, 3], w_in.at[n, 3], left),
        )

    def start_own(n):
        for copy in pack(n):
            copy.wait()
        for copy in own_weights(n):
            copy.start()

    def weights_step(n, ahead=True):
        first, second = relayed_weights(n)
        landed(slot(n, z_prev), w_in.at[n, 0])
        first.start()
        landed(slot(n, z_next), w_in.at[n, 1])
        second.start()
        if ahead:
            @pl.when(n + 2 < chunks)
            def _():
                start_own(n + 2)

    def weights_ready(n):
        far = (z + 2) % 4
        landed(slot(n, far, 0, depth // 2), w_in.at[n, 2])
        landed(slot(n, far, depth // 2, depth // 2), w_in.at[n, 3])

    def block(r, p, j, c):
        return tb.at[
            r,
            pl.ds(pl.multiple_of(p * piece, piece), piece),
            pl.ds(pl.multiple_of(j * 2 * half + c * half, half), half),
        ]

    own_j = b * 2 + yl

    def token_sends(p):
        mine = tok.at[pl.ds(p * piece, piece), :]
        near = [remote(mine, block(1, p, own_j, core), y_out.at[0, p], t_in.at[1, p, own_j], flip)]
        far = [
            remote(mine, block(0, p, own_j, core), y_out.at[0, p], t_in.at[0, p, own_j], cross),
            remote(mine, block(0, p, own_j, core), y_out.at[1, p], t_in.at[0, p, own_j], partner),
        ]
        kept = pltpu.make_async_copy(mine, block(1, p, own_j, core), t_in.at[1, p, own_j])
        return near, far, kept

    def split(i):
        return i // (2 * PIECES), (i % (2 * PIECES)) // 2, i % 2

    def to_sibling(r, p, j, i, g):
        here = block(r, p, j, core)
        return remote(here, here, s_out.at[i, g], t_sib.at[r, p, j], sibling)

    def outward(r, p, j, i, e, to):
        here = block(r, p, j, core)
        return remote(here, here, x_out.at[i, e], t_in.at[r, p, j], to)

    steps = 4 * PIECES

    def near_step(i):
        r, p, q = split(i)
        j = b * 2 + q

        @pl.when(source)
        def _():
            landed(block(r, p, j, core), t_in.at[r, p, j])
            outward(r, p, j, i, 0, pair).start()
            outward(r, p, j, i, 1, outer).start()
            to_sibling(r, p, j, i, 0).start()

    def far_step(i):
        r, p, q = split(i)
        j = (1 - b) * 2 + q
        landed(block(r, p, j, core), t_in.at[r, p, j])

        @pl.when(jnp.logical_not(source))
        def _():
            outward(r, p, j, i, 0, pair).start()

        to_sibling(r, p, j, i, 1).start()

    def last_step(i):
        r, p, q = split(i)
        j = b * 2 + q

        @pl.when(jnp.logical_not(source))
        def _():
            landed(block(r, p, j, core), t_in.at[r, p, j])
            to_sibling(r, p, j, i, 0).start()

    def token_step(i):
        @pl.when(i < steps)
        def _():
            near_step(i)

        @pl.when(jnp.logical_and(i >= 2, i < steps + 2))
        def _():
            far_step(i - 2)

        @pl.when(jnp.logical_and(i >= 3, i < steps + 3))
        def _():
            last_step(i - 3)

    def tokens_ready(r):
        @pl.loop(0, PIECES * 4)
        def _(i):
            p, j = i // 4, i % 4
            landed(block(r, p, j, 1 - core), t_sib.at[r, p, j])

    def product(r, m, n):
        return jnp.dot(
            tb[r, pl.ds(pl.multiple_of(m * piece, piece), piece), :], wb[n], preferred_element_type=jnp.float32
        )

    def partial(n):
        return remote(send.at[n], got.at[n], o_out.at[n], o_in.at[n], partner)

    def send_part(n):
        @pl.loop(0, PIECES)
        def _(m):
            send[n, pl.ds(pl.multiple_of(m * piece, piece), piece), :] = encode(product(0, m, n))

        partial(n).start()

    def own_part(n):
        @pl.loop(0, PIECES)
        def _(m):
            acc[pl.ds(pl.multiple_of(m * piece, piece), piece), :] = product(1, m, n)

        landed(got.at[n], o_in.at[n])

        @pl.loop(0, rows // 32)
        def _(m):
            here = pl.ds(pl.multiple_of(m * 32, 32), 32)
            total = acc[here, :] + decode(got[n, here, :])
            g, u = total[:, :LANES], total[:, LANES:]
            out[here, pl.ds(pl.multiple_of(n * LANES, LANES), LANES)] = (g / (1.0 + jnp.exp(-g)) * u).astype(out.dtype)

    for n in range(chunks):
        for copy in pack(n):
            copy.start()

    barrier = pltpu.get_barrier_semaphore()
    neighbours = (right, left, partner, flip, cross, sibling, pair, outer)
    for to in neighbours:
        pl.semaphore_signal(barrier, inc=1, device_id=to, device_id_type=MESH)
    pl.semaphore_wait(barrier, len(neighbours))

    start_own(0)
    for p in range(PIECES):
        near, far, kept = token_sends(p)

        @pl.when(source)
        def _():
            for copy in near:
                copy.start()
            kept.start()

        @pl.when(jnp.logical_not(source))
        def _():
            for copy in far:
                copy.start()

    start_own(1)

    token_step(jnp.int32(0))
    weights_step(0)
    for i in (1, 2):
        token_step(jnp.int32(i))
    weights_step(1)
    for i in (3, 4, 5):
        token_step(jnp.int32(i))
    weights_step(2)
    for i in (6, 7, 8):
        token_step(jnp.int32(i))
    tokens_ready(0)

    @pl.loop(0, chunks + 1)
    def _(i):
        @pl.when(jnp.logical_and(i >= 2, i + 1 < chunks))
        def _():
            weights_step(i + 1)

        @pl.loop(jnp.where(i == 0, 9, jnp.clip(6 + 3 * i, 9, steps + 3)), jnp.where(i == 0, 9, jnp.clip(9 + 3 * i, 9, steps + 3)))
        def _(s):
            token_step(s)

        @pl.when(i == 3)
        def _():
            tokens_ready(1)

        @pl.when(i < chunks)
        def _():
            weights_ready(i)
            send_part(i)

        @pl.loop(jnp.where(i <= 3, 0, i - 1), jnp.where(i < 3, 0, jnp.where(i == 3, 3, i)))
        def _(n):
            own_part(n)

    @pl.loop(0, chunks)
    def _(n):
        for copy in own_weights(n) + relayed_weights(n):
            copy.wait_send()
        partial(n).wait_send()

    for p in range(PIECES):
        near, far, _ = token_sends(p)

        @pl.when(source)
        def _():
            for copy in near:
                copy.wait_send()

        @pl.when(jnp.logical_not(source))
        def _():
            for copy in far:
                copy.wait_send()

    @pl.loop(0, steps)
    def _(i):
        r, p, q = split(i)
        j = b * 2 + q
        outward(r, p, j, i, 0, pair).wait_send()
        to_sibling(r, p, j, i, 0).wait_send()
        to_sibling(r, p, j, i, 1).wait_send()

        @pl.when(source)
        def _():
            outward(r, p, j, i, 1, outer).wait_send()


def on_device(tokens, gate_weight, up_weight):
    rows, half = tokens.shape
    depth, units = gate_weight.shape
    chunks = units // LANES
    dma = pltpu.SemaphoreType.DMA
    return pl.pallas_call(
        kernel,
        out_shape=jax.ShapeDtypeStruct((rows, units), jnp.bfloat16),
        in_specs=[pl.BlockSpec(memory_space=pl.ANY)] * 3,
        out_specs=pl.BlockSpec(memory_space=pltpu.VMEM),
        scratch_shapes=[
            pltpu.VMEM((chunks, 4 * depth, 2 * LANES), jnp.bfloat16),
            pltpu.VMEM((2, rows, 8 * half), jnp.bfloat16),
            pltpu.VMEM((chunks, rows, 2 * LANES), jnp.bfloat16),
            pltpu.VMEM((chunks, rows, 2 * LANES), jnp.bfloat16),
            pltpu.VMEM((rows, 2 * LANES), jnp.float32),
            dma((chunks, 4)),
            dma((chunks, 4)),
            dma((chunks, 2)),
            dma((2, PIECES, 4)),
            dma((2, PIECES, 4)),
            dma((2, PIECES)),
            dma((4 * PIECES, 2)),
            dma((4 * PIECES, 2)),
            dma((chunks,)),
            dma((chunks,)),
        ],
        compiler_params=pltpu.CompilerParams(
            collective_id=0, has_side_effects=True, vmem_limit_bytes=60 * 2**20
        ),
        cost_estimate=pl.CostEstimate(
            flops=2 * rows * 16 * half * units * 2, bytes_accessed=2 * (rows * half + 2 * depth * units + rows * units), transcendentals=0
        ),
    )(tokens, gate_weight, up_weight)


def solution(mesh):
    placed = (P("row", "col"), P("row", "col"), P("row", "col"))
    return jax.shard_map(
        on_device, mesh=mesh, in_specs=placed, out_specs=P("row", "col"), check_vma=False
    )
```

time: 441 us -> 162 us (0.37)
  waiting for transfers between devices: 390 us -> 0 us
  Pallas kernels: 0 us -> 157 us
  matrix products: 37.2 us -> 0 us
  between operations: 13.1 us -> 0.01 us
    all_gather x3 -> x0, waiting for transfers between devices: 388 us -> none  [the longest x1 167 us: on_device(): lax.all_gather(gate_weight, 'row', axis=0, tiled=True)]
    pallas_call x0 -> x1, Pallas kernels: none -> 157 us  [on_device(): pl.pallas_call(kernel, out_shape=jax.ShapeDtypeStruct((rows, units), jnp....]
    dot_general x2 -> x0, matrix products: 37.2 us -> none  [the longest x1 19.4 us: on_device(): jnp.dot(features, lax.all_gather(up_weight, 'row', axis=0, tiled=True), p...]
  transfers between devices with their start and end apart: 3 -> 0, of which waited for: 3 -> 0; matrix products, arithmetic and copies ran while one was open for 4% -> 0% of each run, Pallas kernels for 0% -> 0%
where the time goes in v1:
time: 162 us; the launch traced here: 159 us
  Pallas kernels  157 us (97%)
  local copies, waits for them, and re-layouts  2.53 us (2%)
    pallas_call x1, Pallas kernels, on_device(): pl.pallas_call(kernel, out_shape=jax.ShapeDtypeStruct((rows, units), jnp....  157 us

profile of v1, /device:TPU:0, one launch (start us, length us, event | category | flops | bytes accessed | tf_op | source)
XLA Modules:
  0.0 159.3 jit_solution(11059249786307905568)
XLA Ops:
  0.0 156.8 %shard_map.37 = bf16[768,896]{1,0:T(8,128)(2,1)} custom-call(bf16[768,512]{1,0:T(8,128)(2,1)} %tok.1, bf16[1024,896]{1,0:T(8,128)(2,1)} %gate.1, bf16[1024,896]{1,0:T(8,128)(2,1)} %up.1), custom_call_target="tpu_custom_call" | custom-call | flops 22548578304 | bytes 5832704 | tf_op jit(solution)/shard_map/pallas_call | solution.py:322
  156.8 2.5 %copy.5 = bf16[768,896]{1,0:T(8,128)(2,1)} copy(bf16[768,896]{1,0:T(8,128)(2,1)} %shard_map.37) | data formatting | bytes 2752512

commit v2 on v1

v2 whole, which is shorter than its diff:
```python
import functools

import jax
import jax.numpy as jnp
from jax import lax
from jax.experimental import pallas as pl
from jax.experimental.pallas import tpu as pltpu
from jax.sharding import PartitionSpec as P

MESH = pl.DeviceIdType.MESH
LANES = 128
PIECES = 3


def encode(v):
    w = v * 2.0**14
    w2 = w * w
    return (w2 * w2 * w).astype(jnp.bfloat16)


def decode(u):
    u = u.astype(jnp.float32)
    r = jnp.exp2(jnp.log2(jnp.abs(u)) * 0.2 - 14.0)
    return jnp.where(u < 0, -r, r)


def kernel(
    tok, gate, up, out,
    wb, tb, send, got, acc,
    w_in, w_out, w_local, t_in, t_sib, y_out, x_out, s_out, o_in, o_out,
):
    rows, half = tok.shape
    depth, units = gate.shape
    chunks = units // LANES
    piece = rows // PIECES
    row, col = lax.axis_index("row"), lax.axis_index("col")
    yh, z = row // 4, row % 4
    x, yl, core = col // 4, (col // 2) % 2, col % 2
    b = x % 2
    source = (x // 2) == yh
    y = yh * 2 + yl

    def at(x=x, y=y, z=z, core=core):
        return ((y // 2) * 4 + z, x * 4 + (y % 2) * 2 + core)

    z_next, z_prev = (z + 1) % 4, (z + 3) % 4
    x_next, x_prev = (x + 1) % 4, (x + 3) % 4
    right, left = at(z=z_next), at(z=z_prev)
    partner = at(y=(y + 2) % 4)
    flip = at(y=yh * 2 + 1 - yl)
    cross = at(y=(1 - yh) * 2 + 1 - yl)
    sibling = at(core=1 - core)
    pair = at(x=jnp.where(b == 0, x_next, x_prev))
    outer = at(x=jnp.where(b == 0, x_prev, x_next))

    def remote(src, dst, ssem, rsem, to):
        return pltpu.make_async_remote_copy(
            src_ref=src, dst_ref=dst, send_sem=ssem, recv_sem=rsem, device_id=to, device_id_type=MESH
        )

    def lines(m, size=piece):
        return pl.ds(pl.multiple_of(m * size, size), size)

    def landed(ref, sem):
        pltpu.make_async_copy(ref, ref, sem).wait()

    def slot(h, s, lo=0, size=depth):
        return wb.at[h, pl.ds(pl.multiple_of(s * depth + lo, size), size), :]

    def pack(n):
        lane = pl.ds(n * LANES, LANES)
        return (
            pltpu.make_async_copy(gate.at[:, lane], slot(2 * n, z), w_local.at[2 * n]),
            pltpu.make_async_copy(up.at[:, lane], slot(2 * n + 1, z), w_local.at[2 * n + 1]),
        )

    def own_weights(h):
        mine = slot(h, z)
        return (
            remote(mine, mine, w_out.at[h, 0], w_in.at[h, 0], right),
            remote(mine, mine, w_out.at[h, 1], w_in.at[h, 1], left),
        )

    def relayed_weights(h):
        top = slot(h, z_prev, 0, depth // 2)
        low = slot(h, z_next, depth // 2, depth // 2)
        return (
            remote(top, top, w_out.at[h, 2], w_in.at[h, 2], right),
            remote(low, low, w_out.at[h, 3], w_in.at[h, 3], left),
        )

    def start_own(h):
        landed(slot(h, z), w_local.at[h])
        for copy in own_weights(h):
            copy.start()

    def weights_step(h):
        first, second = relayed_weights(h)
        landed(slot(h, z_prev), w_in.at[h, 0])
        first.start()
        landed(slot(h, z_next), w_in.at[h, 1])
        second.start()

        @pl.when(h + 2 < 2 * chunks)
        def _():
            start_own(h + 2)

    def weights_ready(h):
        far = (z + 2) % 4
        landed(slot(h, far, 0, depth // 2), w_in.at[h, 2])
        landed(slot(h, far, depth // 2, depth // 2), w_in.at[h, 3])

    def block(r, p, j, c):
        return tb.at[r, p, j, c]

    def tokens_of(r, p):
        return jnp.concatenate([tb[r, p, j, c] for j in range(4) for c in range(2)], axis=1)

    own_j = b * 2 + yl

    def cross_send(p):
        return remote(tok.at[lines(p), :], block(0, p, own_j, core), y_out.at[0, p], t_in.at[0, p, own_j], cross)

    def flip_send(p):
        return remote(tok.at[lines(p), :], block(1, p, own_j, core), y_out.at[1, p], t_in.at[1, p, own_j], flip)

    def flip_pass(p):
        here = block(0, p, b * 2 + 1 - yl, core)
        return remote(here, here, y_out.at[0, p], t_in.at[0, p, b * 2 + 1 - yl], flip)

    def keep(p):
        return pltpu.make_async_copy(tok.at[lines(p), :], block(1, p, own_j, core), t_in.at[1, p, own_j])

    def cross_step(p):
        @pl.when(jnp.logical_not(source))
        def _():
            if p:
                cross_send(p - 1).wait_send()
            cross_send(p).start()

    def flip_step(p):
        @pl.when(source)
        def _():
            flip_send(p).start()

    def near_j(q):
        return b * 2 + (yl + 1 + q) % 2

    def far_j(q):
        return (1 - b) * 2 + (yl + 1 + q) % 2

    def index(r, p, q):
        return (r * PIECES + p) * 2 + q

    def to_sibling(r, p, j, i, g):
        here = block(r, p, j, core)
        return remote(here, here, s_out.at[i, g], t_sib.at[r, p, j], sibling)

    def outward(r, p, j, i, e, to):
        here = block(r, p, j, core)
        return remote(here, here, x_out.at[i, e], t_in.at[r, p, j], to)

    steps = 4 * PIECES

    def near_step(r, p, q):
        i, j = index(r, p, q), near_j(q)

        @pl.when(source)
        def _():
            landed(block(r, p, j, core), t_in.at[r, p, j])
            outward(r, p, j, i, 0, pair).start()
            outward(r, p, j, i, 1, outer).start()
            if isinstance(r, int) and r == 0 and q == 0:
                flip_pass(p).start()
            to_sibling(r, p, j, i, 0).start()

    def far_step(r, p, q):
        i, j = index(r, p, q), far_j(q)
        landed(block(r, p, j, core), t_in.at[r, p, j])

        @pl.when(jnp.logical_not(source))
        def _():
            outward(r, p, j, i, 0, pair).start()

        to_sibling(r, p, j, i, 1).start()

    def last_step(r, p, q):
        i, j = index(r, p, q), near_j(q)

        @pl.when(jnp.logical_not(source))
        def _():
            landed(block(r, p, j, core), t_in.at[r, p, j])
            to_sibling(r, p, j, i, 0).start()

    def own_rows(k):
        return 1, k % PIECES, 1 - k // PIECES

    def tokens_ready(r):
        @pl.loop(0, PIECES * 4)
        def _(i):
            p, j = i // 4, i % 4
            landed(block(r, p, j, 1 - core), t_sib.at[r, p, j])

    def partial(h, m):
        return remote(send.at[h, lines(m)], got.at[h, lines(m)], o_out.at[h, m], o_in.at[h, m], partner)

    def send_part(h):
        weights_ready(h)

        @pl.loop(0, PIECES)
        def _(m):
            part = jnp.dot(tokens_of(0, m), wb[h], preferred_element_type=jnp.float32)
            send[h, lines(m), :] = encode(part)
            partial(h, m).start()

    def own_part(n):
        @pl.loop(0, PIECES)
        def _(m):
            both = jnp.concatenate([wb[2 * n], wb[2 * n + 1]], axis=1)
            acc[lines(m), :] = jnp.dot(tokens_of(1, m), both, preferred_element_type=jnp.float32)

        @pl.loop(0, PIECES)
        def _(m):
            landed(got.at[2 * n, lines(m)], o_in.at[2 * n, m])
            landed(got.at[2 * n + 1, lines(m)], o_in.at[2 * n + 1, m])

            @pl.loop(m * (piece // 32), (m + 1) * (piece // 32))
            def _(t):
                here = lines(t, 32)
                g = acc[here, :LANES] + decode(got[2 * n, here, :])
                u = acc[here, LANES:] + decode(got[2 * n + 1, here, :])
                out[here, pl.ds(pl.multiple_of(n * LANES, LANES), LANES)] = (g / (1.0 + jnp.exp(-g)) * u).astype(out.dtype)

    for n in range(chunks):
        for copy in pack(n):
            copy.start()

    barrier = pltpu.get_barrier_semaphore()
    neighbours = (right, left, partner, flip, cross, sibling, pair, outer)
    for to in neighbours:
        pl.semaphore_signal(barrier, inc=1, device_id=to, device_id_type=MESH)
    pl.semaphore_wait(barrier, len(neighbours))

    start_own(0)
    cross_step(0)

    @pl.when(source)
    def _():
        for p in range(PIECES):
            keep(p).start()

    start_own(1)

    early = (
        ((cross_step, 1), (near_step, 0, 0, 0), (cross_step, 2), (near_step, 0, 1, 0)),
        ((near_step, 0, 0, 1), (far_step, 0, 0, 0), (near_step, 0, 2, 0), (near_step, 0, 1, 1), (far_step, 0, 1, 0), (last_step, 0, 0, 0)),
        ((near_step, 0, 2, 1), (far_step, 0, 0, 1), (last_step, 0, 1, 0), (flip_step, 0)),
        ((far_step, 0, 2, 0), (last_step, 0, 0, 1), (flip_step, 1), (far_step, 0, 1, 1), (last_step, 0, 2, 0), (flip_step, 2)),
        ((near_step, *own_rows(0)), (far_step, 0, 2, 1), (last_step, 0, 1, 1), (near_step, *own_rows(1))),
        ((far_step, *own_rows(0)), (last_step, 0, 2, 1), (near_step, *own_rows(2))),
    )
    for h, events in enumerate(early):
        weights_step(h)
        for event, *which in events:
            event(*which)
    tokens_ready(0)
    late = len(early)

    @pl.loop(late, 2 * chunks + 1)
    def _(h):
        @pl.when(h < 2 * chunks)
        def _():
            weights_step(h)

        @pl.when(h <= 8)
        def _():
            near_step(*own_rows(h - 3))

        @pl.loop(jnp.minimum(h - 5 + jnp.where(h >= 8, 1, 0), 6), jnp.minimum(h - 4 + jnp.where(h >= 7, 1, 0), 6))
        def _(k):
            far_step(*own_rows(k))

        @pl.loop(jnp.minimum(h - 6 + jnp.where(h >= 9, 1, 0), 6), jnp.minimum(h - 5 + jnp.where(h >= 8, 1, 0), 6))
        def _(k):
            last_step(*own_rows(k))

        @pl.when(h == 10)
        def _():
            tokens_ready(1)

        @pl.loop(jnp.where(h == late, 0, jnp.minimum(2 * h - 11, h - 1)), jnp.minimum(2 * h - 9, h))
        def _(s):
            send_part(s)

        @pl.loop(jnp.clip(2 * (h - 10), 0, jnp.maximum(h - 8, 0)), jnp.clip(2 * (h - 9), 0, jnp.maximum(h - 7, 0)))
        def _(n):
            own_part(n)

    @pl.loop(0, 2 * chunks)
    def _(h):
        for copy in own_weights(h) + relayed_weights(h):
            copy.wait_send()

        @pl.loop(0, PIECES)
        def _(m):
            partial(h, m).wait_send()

    for p in range(PIECES):
        @pl.when(source)
        def _():
            flip_pass(p).wait_send()
            flip_send(p).wait_send()

    @pl.when(jnp.logical_not(source))
    def _():
        cross_send(PIECES - 1).wait_send()

    @pl.loop(0, steps)
    def _(i):
        r, p, j = i // (2 * PIECES), (i // 2) % PIECES, b * 2
        outward(r, p, j, i, 0, pair).wait_send()
        to_sibling(r, p, j, i, 0).wait_send()
        to_sibling(r, p, j, i, 1).wait_send()

        @pl.when(source)
        def _():
            outward(r, p, j, i, 1, outer).wait_send()


def on_device(tokens, gate_weight, up_weight):
    rows, half = tokens.shape
    depth, units = gate_weight.shape
    chunks = units // LANES
    dma = pltpu.SemaphoreType.DMA
    return pl.pallas_call(
        kernel,
        out_shape=jax.ShapeDtypeStruct((rows, units), jnp.bfloat16),
        in_specs=[pl.BlockSpec(memory_space=pl.ANY)] * 3,
        out_specs=pl.BlockSpec(memory_space=pltpu.VMEM),
        scratch_shapes=[
            pltpu.VMEM((2 * chunks, 4 * depth, LANES), jnp.bfloat16),
            pltpu.VMEM((2, PIECES, 4, 2, rows // PIECES, half), jnp.bfloat16),
            pltpu.VMEM((2 * chunks, rows, LANES), jnp.bfloat16),
            pltpu.VMEM((2 * chunks, rows, LANES), jnp.bfloat16),
            pltpu.VMEM((rows, 2 * LANES), jnp.float32),
            dma((2 * chunks, 4)),
            dma((2 * chunks, 4)),
            dma((2 * chunks,)),
            dma((2, PIECES, 4)),
            dma((2, PIECES, 4)),
            dma((2, PIECES)),
            dma((4 * PIECES, 2)),
            dma((4 * PIECES, 2)),
            dma((2 * chunks, PIECES)),
            dma((2 * chunks, PIECES)),
        ],
        compiler_params=pltpu.CompilerParams(
            collective_id=0, has_side_effects=True, vmem_limit_bytes=60 * 2**20
        ),
        cost_estimate=pl.CostEstimate(
            flops=2 * rows * 16 * half * units * 2, bytes_accessed=2 * (rows * half + 2 * depth * units + rows * units), transcendentals=0
        ),
    )(tokens, gate_weight, up_weight)


def solution(mesh):
    placed = (P("row", "col"), P("row", "col"), P("row", "col"))
    return jax.shard_map(
        on_device, mesh=mesh, in_specs=placed, out_specs=P("row", "col"), check_vma=False
    )
```

time: 162 us -> 144 us (0.89); the launches traced: 159 us -> 144 us
  Pallas kernels: 157 us -> 141 us
    pallas_call x1, Pallas kernels: 157 us -> 141 us  [on_device(): pl.pallas_call(kernel, out_shape=jax.ShapeDtypeStruct((rows, units), jnp....]
where the time goes in v2:
time: 144 us
  Pallas kernels  141 us (98%)
  local copies, waits for them, and re-layouts  2.53 us (2%)
    pallas_call x1, Pallas kernels, on_device(): pl.pallas_call(kernel, out_shape=jax.ShapeDtypeStruct((rows, units), jnp....  141 us

profile of v2, /device:TPU:0, one launch (start us, length us, event | category | flops | bytes accessed | tf_op | source)
XLA Modules:
  0.0 143.9 jit_solution(5308450755796404776)
XLA Ops:
  0.0 141.4 %shard_map.37 = bf16[768,896]{1,0:T(8,128)(2,1)} custom-call(bf16[768,512]{1,0:T(8,128)(2,1)} %tok.1, bf16[1024,896]{1,0:T(8,128)(2,1)} %gate.1, bf16[1024,896]{1,0:T(8,128)(2,1)} %up.1), custom_call_target="tpu_custom_call" | custom-call | flops 22548578304 | bytes 5832704 | tf_op jit(solution)/shard_map/pallas_call | solution.py:335
  141.4 2.5 %copy.5 = bf16[768,896]{1,0:T(8,128)(2,1)} copy(bf16[768,896]{1,0:T(8,128)(2,1)} %shard_map.37) | data formatting | bytes 2752512

commit v3 on v2

--- a/solution.py
+++ b/solution.py
@@ -25,9 +25,9 @@
 
 
 def kernel(
-    tok, gate, up, out,
-    wb, tb, send, got, acc,
-    w_in, w_out, w_local, t_in, t_sib, y_out, x_out, s_out, o_in, o_out,
+    tok, gate, up, out_hbm,
+    wb, tb, send, got, acc, out,
+    w_in, w_out, w_local, t_in, t_sib, y_out, x_out, s_out, o_in, o_out, done,
 ):
     rows, half = tok.shape
     depth, units = gate.shape
@@ -74,41 +74,58 @@
             pltpu.make_async_copy(up.at[:, lane], slot(2 * n + 1, z), w_local.at[2 * n + 1]),
         )
 
-    def own_weights(h):
-        mine = slot(h, z)
+    def first_half(h):
+        top, low = slot(h, z, 0, depth // 2), slot(h, z, depth // 2, depth // 2)
         return (
-            remote(mine, mine, w_out.at[h, 0], w_in.at[h, 0], right),
-            remote(mine, mine, w_out.at[h, 1], w_in.at[h, 1], left),
+            remote(top, top, w_out.at[h, 0], w_in.at[h, 0], right),
+            remote(low, low, w_out.at[h, 1], w_in.at[h, 1], left),
         )
 
-    def relayed_weights(h):
+    def second_half(h):
+        top, low = slot(h, z, 0, depth // 2), slot(h, z, depth // 2, depth // 2)
+        return (
+            remote(low, low, w_out.at[h, 2], w_in.at[h, 2], right),
+            remote(top, top, w_out.at[h, 3], w_in.at[h, 3], left),
+        )
+
+    def relayed(h):
         top = slot(h, z_prev, 0, depth // 2)
         low = slot(h, z_next, depth // 2, depth // 2)
         return (
-            remote(top, top, w_out.at[h, 2], w_in.at[h, 2], right),
-            remote(low, low, w_out.at[h, 3], w_in.at[h, 3], left),
+            remote(top, top, w_out.at[h, 4], w_in.at[h, 4], right),
+            remote(low, low, w_out.at[h, 5], w_in.at[h, 5], left),
         )
 
-    def start_own(h):
+    def start_first(h):
         landed(slot(h, z), w_local.at[h])
-        for copy in own_weights(h):
+        for copy in first_half(h):
             copy.start()
 
+    def start_second(h):
+        for copy in second_half(h):
+            copy.start()
+
     def weights_step(h):
-        first, second = relayed_weights(h)
-        landed(slot(h, z_prev), w_in.at[h, 0])
+        first, second = relayed(h)
+        landed(slot(h, z_prev, 0, depth // 2), w_in.at[h, 0])
         first.start()
-        landed(slot(h, z_next), w_in.at[h, 1])
+        landed(slot(h, z_next, depth // 2, depth // 2), w_in.at[h, 1])
         second.start()
 
+        @pl.when(h + 1 < 2 * chunks)
+        def _():
+            start_second(h + 1)
+
         @pl.when(h + 2 < 2 * chunks)
         def _():
-            start_own(h + 2)
+            start_first(h + 2)
 
     def weights_ready(h):
         far = (z + 2) % 4
-        landed(slot(h, far, 0, depth // 2), w_in.at[h, 2])
-        landed(slot(h, far, depth // 2, depth // 2), w_in.at[h, 3])
+        landed(slot(h, z_prev, depth // 2, depth // 2), w_in.at[h, 2])
+        landed(slot(h, z_next, 0, depth // 2), w_in.at[h, 3])
+        landed(slot(h, far, 0, depth // 2), w_in.at[h, 4])
+        landed(slot(h, far, depth // 2, depth // 2), w_in.at[h, 5])
 
     def block(r, p, j, c):
         return tb.at[r, p, j, c]
@@ -229,7 +246,13 @@
                 here = lines(t, 32)
                 g = acc[here, :LANES] + decode(got[2 * n, here, :])
                 u = acc[here, LANES:] + decode(got[2 * n + 1, here, :])
-                out[here, pl.ds(pl.multiple_of(n * LANES, LANES), LANES)] = (g / (1.0 + jnp.exp(-g)) * u).astype(out.dtype)
+                out[n, here, :] = (g / (1.0 + jnp.exp(-g)) * u).astype(out.dtype)
+
+            result(n, m).start()
+
+    def result(n, m):
+        lane = pl.ds(pl.multiple_of(n * LANES, LANES), LANES)
+        return pltpu.make_async_copy(out.at[n, lines(m)], out_hbm.at[lines(m), lane], done.at[n, m])
 
     for n in range(chunks):
         for copy in pack(n):
@@ -241,7 +264,8 @@
         pl.semaphore_signal(barrier, inc=1, device_id=to, device_id_type=MESH)
     pl.semaphore_wait(barrier, len(neighbours))
 
-    start_own(0)
+    start_first(0)
+    start_second(0)
     cross_step(0)
 
     @pl.when(source)
@@ -249,7 +273,7 @@
         for p in range(PIECES):
             keep(p).start()
 
-    start_own(1)
+    start_first(1)
 
     early = (
         ((cross_step, 1), (near_step, 0, 0, 0), (cross_step, 2), (near_step, 0, 1, 0)),
@@ -298,12 +322,18 @@
 
     @pl.loop(0, 2 * chunks)
     def _(h):
-        for copy in own_weights(h) + relayed_weights(h):
+        for copy in first_half(h) + second_half(h) + relayed(h):
             copy.wait_send()
 
         @pl.loop(0, PIECES)
         def _(m):
             partial(h, m).wait_send()
+
+    @pl.loop(0, chunks)
+    def _(n):
+        @pl.loop(0, PIECES)
+        def _(m):
+            result(n, m).wait()
 
     for p in range(PIECES):
         @pl.when(source)
@@ -336,15 +366,16 @@
         kernel,
         out_shape=jax.ShapeDtypeStruct((rows, units), jnp.bfloat16),
         in_specs=[pl.BlockSpec(memory_space=pl.ANY)] * 3,
-        out_specs=pl.BlockSpec(memory_space=pltpu.VMEM),
+        out_specs=pl.BlockSpec(memory_space=pl.ANY),
         scratch_shapes=[
             pltpu.VMEM((2 * chunks, 4 * depth, LANES), jnp.bfloat16),
             pltpu.VMEM((2, PIECES, 4, 2, rows // PIECES, half), jnp.bfloat16),
             pltpu.VMEM((2 * chunks, rows, LANES), jnp.bfloat16),
             pltpu.VMEM((2 * chunks, rows, LANES), jnp.bfloat16),
             pltpu.VMEM((rows, 2 * LANES), jnp.float32),
-            dma((2 * chunks, 4)),
-            dma((2 * chunks, 4)),
+            pltpu.VMEM((chunks, rows, LANES), jnp.bfloat16),
+            dma((2 * chunks, 6)),
+            dma((2 * chunks, 6)),
             dma((2 * chunks,)),
             dma((2, PIECES, 4)),
             dma((2, PIECES, 4)),
@@ -353,6 +384,7 @@
             dma((4 * PIECES, 2)),
             dma((2 * chunks, PIECES)),
             dma((2 * chunks, PIECES)),
+            dma((chunks, PIECES)),
         ],
         compiler_params=pltpu.CompilerParams(
             collective_id=0, has_side_effects=True, vmem_limit_bytes=60 * 2**20

time: 144 us -> 141 us (0.979)
  Pallas kernels: 141 us -> 138 us
    pallas_call x1, Pallas kernels: 141 us -> 138 us  [on_device(): pl.pallas_call(kernel, out_shape=jax.ShapeDtypeStruct((rows, units), jnp....]
where the time goes in v3:
time: 141 us
  Pallas kernels  138 us (98%)
  local copies, waits for them, and re-layouts  2.53 us (2%)
    pallas_call x1, Pallas kernels, on_device(): pl.pallas_call(kernel, out_shape=jax.ShapeDtypeStruct((rows, units), jnp....  138 us

profile of v3, /device:TPU:0, one launch (start us, length us, event | category | flops | bytes accessed | tf_op | source)
XLA Modules:
  0.0 140.9 jit_solution(18351349590186671296)
XLA Ops:
  0.0 138.3 %shard_map.37 = bf16[768,896]{1,0:T(8,128)(2,1)} custom-call(bf16[768,512]{1,0:T(8,128)(2,1)} %tok.1, bf16[1024,896]{1,0:T(8,128)(2,1)} %gate.1, bf16[1024,896]{1,0:T(8,128)(2,1)} %up.1), custom_call_target="tpu_custom_call" | custom-call | flops 22548578304 | bytes 5832704 | tf_op jit(solution)/shard_map/pallas_call | solution.py:365
  138.4 2.5 %copy.5 = bf16[768,896]{1,0:T(8,128)(2,1)} copy(bf16[768,896]{1,0:T(8,128)(2,1)} %shard_map.37) | data formatting | bytes 2752512

commit v4 on v3

--- a/solution.py
+++ b/solution.py
@@ -25,9 +25,9 @@
 
 
 def kernel(
-    tok, gate, up, out_hbm,
+    tok, gate, up, hidden, last_own, last_got,
     wb, tb, send, got, acc, out,
-    w_in, w_out, w_local, t_in, t_sib, y_out, x_out, s_out, o_in, o_out, done,
+    w_in, w_out, w_local, t_in, t_sib, y_out, x_out, s_out, o_in, o_out, done, kept,
 ):
     rows, half = tok.shape
     depth, units = gate.shape
@@ -218,9 +218,15 @@
             p, j = i // 4, i % 4
             landed(block(r, p, j, 1 - core), t_sib.at[r, p, j])
 
+    last = 2 * chunks - 2
+
     def partial(h, m):
         return remote(send.at[h, lines(m)], got.at[h, lines(m)], o_out.at[h, m], o_in.at[h, m], partner)
 
+    def last_partial(g, m):
+        h = last + g
+        return remote(send.at[h, lines(m)], last_got.at[g, lines(m)], o_out.at[h, m], o_in.at[h, m], partner)
+
     def send_part(h):
         weights_ready(h)
 
@@ -228,7 +234,46 @@
         def _(m):
             part = jnp.dot(tokens_of(0, m), wb[h], preferred_element_type=jnp.float32)
             send[h, lines(m), :] = encode(part)
-            partial(h, m).start()
+
+            @pl.when(h < last)
+            def _():
+                partial(h, m).start()
+
+            @pl.when(h == last)
+            def _():
+                last_partial(0, m).start()
+
+    def last_send_part():
+        h = 2 * chunks - 1
+        far = (z + 2) % 4
+        landed(slot(h, z_prev, depth // 2, depth // 2), w_in.at[h, 2])
+        landed(slot(h, z_next, 0, depth // 2), w_in.at[h, 3])
+
+        def some(m, s):
+            rows_of = jnp.concatenate([tb[0, m, s, c] for c in range(2)], axis=1)
+            return jnp.dot(rows_of, wb[h, pl.ds(pl.multiple_of(s * depth, depth), depth), :], preferred_element_type=jnp.float32)
+
+        @pl.loop(0, PIECES)
+        def _(m):
+            acc[lines(m), :LANES] = some(m, z) + some(m, z_prev) + some(m, z_next)
+
+        landed(slot(h, far, 0, depth // 2), w_in.at[h, 4])
+        landed(slot(h, far, depth // 2, depth // 2), w_in.at[h, 5])
+
+        @pl.loop(0, PIECES)
+        def _(m):
+            send[h, lines(m), :] = encode(acc[lines(m), :LANES] + some(m, far))
+            last_partial(1, m).start()
+
+    def last_own_part():
+        @pl.loop(0, PIECES)
+        def _(m):
+            both = jnp.concatenate([wb[last], wb[last + 1]], axis=1)
+            acc[lines(m), :] = jnp.dot(tokens_of(1, m), both, preferred_element_type=jnp.float32)
+            kept_sums(m).start()
+
+    def kept_sums(m):
+        return pltpu.make_async_copy(acc.at[lines(m)], last_own.at[lines(m)], kept.at[m])
 
     def own_part(n):
         @pl.loop(0, PIECES)
@@ -252,7 +297,7 @@
 
     def result(n, m):
         lane = pl.ds(pl.multiple_of(n * LANES, LANES), LANES)
-        return pltpu.make_async_copy(out.at[n, lines(m)], out_hbm.at[lines(m), lane], done.at[n, m])
+        return pltpu.make_async_copy(out.at[n, lines(m)], hidden.at[lines(m), lane], done.at[n, m])
 
     for n in range(chunks):
         for copy in pack(n):
@@ -290,11 +335,9 @@
     tokens_ready(0)
     late = len(early)
 
-    @pl.loop(late, 2 * chunks + 1)
+    @pl.loop(late, 2 * chunks)
     def _(h):
-        @pl.when(h < 2 * chunks)
-        def _():
-            weights_step(h)
+        weights_step(h)
 
         @pl.when(h <= 8)
         def _():
@@ -316,20 +359,26 @@
         def _(s):
             send_part(s)
 
-        @pl.loop(jnp.clip(2 * (h - 10), 0, jnp.maximum(h - 8, 0)), jnp.clip(2 * (h - 9), 0, jnp.maximum(h - 7, 0)))
+        @pl.loop(jnp.clip(2 * (h - 10), 0, jnp.clip(h - 8, 0, 5)), jnp.where(h == 13, 5, jnp.clip(2 * (h - 9), 0, jnp.maximum(h - 7, 0))))
         def _(n):
             own_part(n)
+
+    last_send_part()
+    own_part(chunks - 2)
+    last_own_part()
 
     @pl.loop(0, 2 * chunks)
     def _(h):
         for copy in first_half(h) + second_half(h) + relayed(h):
             copy.wait_send()
 
-        @pl.loop(0, PIECES)
-        def _(m):
-            partial(h, m).wait_send()
-
-    @pl.loop(0, chunks)
+        @pl.when(h < last)
+        def _():
+            @pl.loop(0, PIECES)
+            def _(m):
+                partial(h, m).wait_send()
+
+    @pl.loop(0, chunks - 1)
     def _(n):
         @pl.loop(0, PIECES)
         def _(m):
@@ -356,17 +405,66 @@
         def _():
             outward(r, p, j, i, 1, outer).wait_send()
 
+    for m in range(PIECES):
+        kept_sums(m).wait()
+        for g in range(2):
+            last_partial(g, m).wait_send()
+            landed(last_got.at[g, lines(m)], o_in.at[last + g, m])
+
+
+def closing(hidden, last_own, last_got, out, whole, own, got, sem_in, sem_out):
+    rows, units = out.shape
+    piece = rows // PIECES
+    known = units - LANES
+
+    def lines(m):
+        return pl.ds(m * piece, piece)
+
+    def loads(m):
+        return (
+            pltpu.make_async_copy(last_own.at[lines(m)], own.at[lines(m)], sem_in.at[m, 0]),
+            pltpu.make_async_copy(last_got.at[0, lines(m)], got.at[0, lines(m)], sem_in.at[m, 1]),
+            pltpu.make_async_copy(last_got.at[1, lines(m)], got.at[1, lines(m)], sem_in.at[m, 2]),
+            pltpu.make_async_copy(hidden.at[lines(m)], whole.at[lines(m), pl.ds(0, known)], sem_in.at[m, 3]),
+        )
+
+    def store(m):
+        return pltpu.make_async_copy(whole.at[lines(m)], out.at[lines(m)], sem_out.at[m])
+
+    for m in range(PIECES):
+        for copy in loads(m):
+            copy.start()
+    for m in range(PIECES):
+        for copy in loads(m):
+            copy.wait()
+
+        @pl.loop(m * (piece // 32), (m + 1) * (piece // 32))
+        def _(t):
+            here = pl.ds(pl.multiple_of(t * 32, 32), 32)
+            g = own[here, :LANES] + decode(got[0, here, :])
+            u = own[here, LANES:] + decode(got[1, here, :])
+            whole[here, pl.ds(known, LANES)] = (g / (1.0 + jnp.exp(-g)) * u).astype(out.dtype)
+
+        store(m).start()
+    for m in range(PIECES):
+        store(m).wait()
+
 
 def on_device(tokens, gate_weight, up_weight):
     rows, half = tokens.shape
     depth, units = gate_weight.shape
     chunks = units // LANES
     dma = pltpu.SemaphoreType.DMA
-    return pl.pallas_call(
+    any_space = pl.BlockSpec(memory_space=pl.ANY)
+    parts = pl.pallas_call(
         kernel,
-        out_shape=jax.ShapeDtypeStruct((rows, units), jnp.bfloat16),
-        in_specs=[pl.BlockSpec(memory_space=pl.ANY)] * 3,
-        out_specs=pl.BlockSpec(memory_space=pl.ANY),
+        out_shape=(
+            jax.ShapeDtypeStruct((rows, units - LANES), jnp.bfloat16),
+            jax.ShapeDtypeStruct((rows, 2 * LANES), jnp.float32),
+            jax.ShapeDtypeStruct((2, rows, LANES), jnp.bfloat16),
+        ),
+        in_specs=[any_space] * 3,
+        out_specs=(any_space,) * 3,
         scratch_shapes=[
             pltpu.VMEM((2 * chunks, 4 * depth, LANES), jnp.bfloat16),
             pltpu.VMEM((2, PIECES, 4, 2, rows // PIECES, half), jnp.bfloat16),
@@ -385,6 +483,7 @@
             dma((2 * chunks, PIECES)),
             dma((2 * chunks, PIECES)),
             dma((chunks, PIECES)),
+            dma((PIECES,)),
         ],
         compiler_params=pltpu.CompilerParams(
             collective_id=0, has_side_effects=True, vmem_limit_bytes=60 * 2**20
@@ -393,6 +492,19 @@
             flops=2 * rows * 16 * half * units * 2, bytes_accessed=2 * (rows * half + 2 * depth * units + rows * units), transcendentals=0
         ),
     )(tokens, gate_weight, up_weight)
+    return pl.pallas_call(
+        closing,
+        out_shape=jax.ShapeDtypeStruct((rows, units), jnp.bfloat16),
+        in_specs=[any_space] * 3,
+        out_specs=any_space,
+        scratch_shapes=[
+            pltpu.VMEM((rows, units), jnp.bfloat16),
+            pltpu.VMEM((rows, 2 * LANES), jnp.float32),
+            pltpu.VMEM((2, rows, LANES), jnp.bfloat16),
+            dma((PIECES, 4)),
+            dma((PIECES,)),
+        ],
+    )(*parts)
 
 
 def solution(mesh):

time: 141 us -> 140 us (level)
  local copies, waits for them, and re-layouts: 2.53 us -> 0 us
    unnamed x1 -> x0, local copies, waits for them, and re-layouts: 2.53 us -> none
    pallas_call x1 -> x2, Pallas kernels: 138 us -> 139 us  [the longest x1 136 us: on_device(): pl.pallas_call(kernel, out_shape=(jax.ShapeDtypeStruct((rows, units - LAN...]
where the time goes in v4:
time: 140 us
  Pallas kernels  139 us (99%)
    pallas_call x1, Pallas kernels, on_device(): pl.pallas_call(kernel, out_shape=(jax.ShapeDtypeStruct((rows, units - LAN...  136 us
    pallas_call x1, Pallas kernels, on_device(): pl.pallas_call(closing, out_shape=jax.ShapeDtypeStruct((rows, units), jnp...  3.04 us

profile of v4, /device:TPU:0, one launch (start us, length us, event | category | flops | bytes accessed | tf_op | source)
XLA Modules:
  0.0 139.5 jit_solution(11436090468248511536)
XLA Ops:
  0.0 136.5 %shard_map.37 = (bf16[768,768]{1,0:T(8,128)(2,1)}, f32[768,256]{1,0:T(8,128)}, bf16[2,768,128]{2,1,0:T(8,128)(2,1)}) custom-call(bf16[768,512]{1,0:T(8,128)(2,1)} %tok.1, bf16[1024,896]{1,0:T(8,128)(2,1)} %gate.1, bf16[1024,896]{1,0:T(8,128)(2,1)} %up.1), custom_call_target="tpu_custom_call" | custom-call | flops 22548578304 | bytes 5832704 | tf_op jit(solution)/shard_map/pallas_call | solution.py:459
  136.5 3.0 %shard_map.38 = bf16[768,896]{1,0:T(8,128)(2,1)} custom-call(bf16[768,768]{1,0:T(8,128)(2,1)} %get-tuple-element.8.hidden, f32[768,256]{1,0:T(8,128)} %get-tuple-element.9.last_own, bf16[2,768,128]{2,1,0:T(8,128)(2,1)} %get-tuple-element.10.last_got), custom_call_target="tpu_custom_call" | custom-call | tf_op jit(solution)/shard_map/pallas_call | solution.py:495

commit v5 on v4

--- a/solution.py
+++ b/solution.py
@@ -25,14 +25,15 @@
 
 
 def kernel(
-    tok, gate, up, hidden, last_own, last_got,
-    wb, tb, send, got, acc, out,
+    tok, gate, up, hidden, last_own_sums, last_got,
+    wb, tb, send, got, acc, ahead, out,
     w_in, w_out, w_local, t_in, t_sib, y_out, x_out, s_out, o_in, o_out, done, kept,
 ):
     rows, half = tok.shape
     depth, units = gate.shape
     chunks = units // LANES
     piece = rows // PIECES
+    last = 2 * chunks - 2
     row, col = lax.axis_index("row"), lax.axis_index("col")
     yh, z = row // 4, row % 4
     x, yl, core = col // 4, (col // 2) % 2, col % 2
@@ -112,11 +113,15 @@
         landed(slot(h, z_next, depth // 2, depth // 2), w_in.at[h, 1])
         second.start()
 
+        @pl.when(h == last)
+        def _():
+            start_first(h + 1)
+
         @pl.when(h + 1 < 2 * chunks)
         def _():
             start_second(h + 1)
 
-        @pl.when(h + 2 < 2 * chunks)
+        @pl.when(h + 2 < 2 * chunks - 1)
         def _():
             start_first(h + 2)
 
@@ -210,15 +215,11 @@
             to_sibling(r, p, j, i, 0).start()
 
     def own_rows(k):
-        return 1, k % PIECES, 1 - k // PIECES
-
-    def tokens_ready(r):
-        @pl.loop(0, PIECES * 4)
-        def _(i):
-            p, j = i // 4, i % 4
+        return 1, k // 2, 1 - k % 2
+
+    def tokens_ready(r, p):
+        for j in range(4):
             landed(block(r, p, j, 1 - core), t_sib.at[r, p, j])
-
-    last = 2 * chunks - 2
 
     def partial(h, m):
         return remote(send.at[h, lines(m)], got.at[h, lines(m)], o_out.at[h, m], o_in.at[h, m], partner)
@@ -226,6 +227,20 @@
     def last_partial(g, m):
         h = last + g
         return remote(send.at[h, lines(m)], last_got.at[g, lines(m)], o_out.at[h, m], o_in.at[h, m], partner)
+
+    def both(n):
+        return jnp.concatenate([wb[2 * n], wb[2 * n + 1]], axis=1)
+
+    def send_pair(n):
+        weights_ready(2 * n)
+        weights_ready(2 * n + 1)
+
+        @pl.loop(0, PIECES)
+        def _(m):
+            part = jnp.dot(tokens_of(0, m), both(n), preferred_element_type=jnp.float32)
+            for g in range(2):
+                send[2 * n + g, lines(m), :] = encode(part[:, g * LANES : (g + 1) * LANES])
+                partial(2 * n + g, m).start()
 
     def send_part(h):
         weights_ready(h)
@@ -243,70 +258,65 @@
             def _():
                 last_partial(0, m).start()
 
-    def last_send_part():
-        h = 2 * chunks - 1
-        far = (z + 2) % 4
-        landed(slot(h, z_prev, depth // 2, depth // 2), w_in.at[h, 2])
-        landed(slot(h, z_next, 0, depth // 2), w_in.at[h, 3])
-
-        def some(m, s):
-            rows_of = jnp.concatenate([tb[0, m, s, c] for c in range(2)], axis=1)
-            return jnp.dot(rows_of, wb[h, pl.ds(pl.multiple_of(s * depth, depth), depth), :], preferred_element_type=jnp.float32)
+    def some(m, s):
+        rows_of = jnp.concatenate([tb[0, m, s, c] for c in range(2)], axis=1)
+        return jnp.dot(rows_of, wb[last + 1, pl.ds(pl.multiple_of(s * depth, depth), depth), :], preferred_element_type=jnp.float32)
+
+    def last_up_ahead():
+        landed(slot(last + 1, z_prev, depth // 2, depth // 2), w_in.at[last + 1, 2])
+        landed(slot(last + 1, z_next, 0, depth // 2), w_in.at[last + 1, 3])
 
         @pl.loop(0, PIECES)
         def _(m):
-            acc[lines(m), :LANES] = some(m, z) + some(m, z_prev) + some(m, z_next)
-
-        landed(slot(h, far, 0, depth // 2), w_in.at[h, 4])
-        landed(slot(h, far, depth // 2, depth // 2), w_in.at[h, 5])
+            ahead[lines(m), :] = some(m, z) + some(m, z_prev) + some(m, z_next)
+
+    def last_up():
+        far = (z + 2) % 4
+        landed(slot(last + 1, far, 0, depth // 2), w_in.at[last + 1, 4])
+        landed(slot(last + 1, far, depth // 2, depth // 2), w_in.at[last + 1, 5])
 
         @pl.loop(0, PIECES)
         def _(m):
-            send[h, lines(m), :] = encode(acc[lines(m), :LANES] + some(m, far))
+            send[last + 1, lines(m), :] = encode(ahead[lines(m), :] + some(m, far))
             last_partial(1, m).start()
 
-    def last_own_part():
+    def last_own(g):
         @pl.loop(0, PIECES)
         def _(m):
-            both = jnp.concatenate([wb[last], wb[last + 1]], axis=1)
-            acc[lines(m), :] = jnp.dot(tokens_of(1, m), both, preferred_element_type=jnp.float32)
-            kept_sums(m).start()
-
-    def kept_sums(m):
-        return pltpu.make_async_copy(acc.at[lines(m)], last_own.at[lines(m)], kept.at[m])
-
-    def own_part(n):
-        @pl.loop(0, PIECES)
-        def _(m):
-            both = jnp.concatenate([wb[2 * n], wb[2 * n + 1]], axis=1)
-            acc[lines(m), :] = jnp.dot(tokens_of(1, m), both, preferred_element_type=jnp.float32)
-
-        @pl.loop(0, PIECES)
-        def _(m):
-            landed(got.at[2 * n, lines(m)], o_in.at[2 * n, m])
-            landed(got.at[2 * n + 1, lines(m)], o_in.at[2 * n + 1, m])
-
-            @pl.loop(m * (piece // 32), (m + 1) * (piece // 32))
-            def _(t):
-                here = lines(t, 32)
-                g = acc[here, :LANES] + decode(got[2 * n, here, :])
-                u = acc[here, LANES:] + decode(got[2 * n + 1, here, :])
-                out[n, here, :] = (g / (1.0 + jnp.exp(-g)) * u).astype(out.dtype)
-
-            result(n, m).start()
+            acc[lines(m), pl.ds(g * LANES, LANES)] = jnp.dot(tokens_of(1, m), wb[last + g], preferred_element_type=jnp.float32)
+            kept_sums(g, m).start()
+
+    def kept_sums(g, m):
+        lane = pl.ds(g * LANES, LANES)
+        return pltpu.make_async_copy(acc.at[lines(m), lane], last_own_sums.at[lines(m), lane], kept.at[g, m])
+
+    def own_product(n, m):
+        acc[lines(m), :] = jnp.dot(tokens_of(1, m), both(n), preferred_element_type=jnp.float32)
+
+    def own_finish(n, m):
+        landed(got.at[2 * n, lines(m)], o_in.at[2 * n, m])
+        landed(got.at[2 * n + 1, lines(m)], o_in.at[2 * n + 1, m])
+
+        @pl.loop(m * (piece // 32), (m + 1) * (piece // 32))
+        def _(t):
+            here = lines(t, 32)
+            g = acc[here, :LANES] + decode(got[2 * n, here, :])
+            u = acc[here, LANES:] + decode(got[2 * n + 1, here, :])
+            out[n, here, :] = (g / (1.0 + jnp.exp(-g)) * u).astype(out.dtype)
+
+        result(n, m).start()
 
     def result(n, m):
         lane = pl.ds(pl.multiple_of(n * LANES, LANES), LANES)
         return pltpu.make_async_copy(out.at[n, lines(m)], hidden.at[lines(m), lane], done.at[n, m])
-
-    for n in range(chunks):
-        for copy in pack(n):
-            copy.start()
 
     barrier = pltpu.get_barrier_semaphore()
     neighbours = (right, left, partner, flip, cross, sibling, pair, outer)
     for to in neighbours:
         pl.semaphore_signal(barrier, inc=1, device_id=to, device_id_type=MESH)
+    for n in range(chunks):
+        for copy in pack(n):
+            copy.start()
     pl.semaphore_wait(barrier, len(neighbours))
 
     start_first(0)
@@ -324,48 +334,72 @@
         ((cross_step, 1), (near_step, 0, 0, 0), (cross_step, 2), (near_step, 0, 1, 0)),
         ((near_step, 0, 0, 1), (far_step, 0, 0, 0), (near_step, 0, 2, 0), (near_step, 0, 1, 1), (far_step, 0, 1, 0), (last_step, 0, 0, 0)),
         ((near_step, 0, 2, 1), (far_step, 0, 0, 1), (last_step, 0, 1, 0), (flip_step, 0)),
-        ((far_step, 0, 2, 0), (last_step, 0, 0, 1), (flip_step, 1), (far_step, 0, 1, 1), (last_step, 0, 2, 0), (flip_step, 2)),
-        ((near_step, *own_rows(0)), (far_step, 0, 2, 1), (last_step, 0, 1, 1), (near_step, *own_rows(1))),
-        ((far_step, *own_rows(0)), (last_step, 0, 2, 1), (near_step, *own_rows(2))),
+        ((near_step, *own_rows(0)), (far_step, 0, 2, 0), (last_step, 0, 0, 1), (flip_step, 1), (far_step, 0, 1, 1), (last_step, 0, 2, 0), (flip_step, 2)),
+        ((near_step, *own_rows(1)), (near_step, *own_rows(2)), (far_step, 0, 2, 1), (last_step, 0, 1, 1)),
+        ((last_step, 0, 2, 1), *((near_step, *own_rows(k)) for k in (3, 4, 5)), (far_step, *own_rows(0))),
     )
     for h, events in enumerate(early):
         weights_step(h)
         for event, *which in events:
             event(*which)
-    tokens_ready(0)
+    for p in range(PIECES):
+        tokens_ready(0, p)
     late = len(early)
 
-    @pl.loop(late, 2 * chunks)
+    def unit(k):
+        return jnp.where(k < 9, k % 3, 3 + (k - 9) // 3), jnp.where(k < 9, k // 3, (k - 9) % 3)
+
+    def steps_at(h, counts):
+        done = [jnp.int32(0)] + [jnp.int32(c) for c in counts]
+        lo, hi = done[0], done[1]
+        for i in range(1, len(counts)):
+            lo = jnp.where(h >= late + i, done[i], lo)
+            hi = jnp.where(h >= late + i, done[i + 1], hi)
+        return lo, hi
+
+    @pl.loop(late, last + 2)
     def _(h):
         weights_step(h)
 
-        @pl.when(h <= 8)
-        def _():
-            near_step(*own_rows(h - 3))
-
-        @pl.loop(jnp.minimum(h - 5 + jnp.where(h >= 8, 1, 0), 6), jnp.minimum(h - 4 + jnp.where(h >= 7, 1, 0), 6))
+        @pl.loop(*steps_at(h, (1, 3, 4, 5, 5, 5, 5, 5)))
         def _(k):
-            far_step(*own_rows(k))
-
-        @pl.loop(jnp.minimum(h - 6 + jnp.where(h >= 9, 1, 0), 6), jnp.minimum(h - 5 + jnp.where(h >= 8, 1, 0), 6))
+            far_step(*own_rows(k + 1))
+
+        @pl.loop(*steps_at(h, (1, 2, 4, 5, 6, 6, 6, 6)))
         def _(k):
             last_step(*own_rows(k))
 
-        @pl.when(h == 10)
-        def _():
-            tokens_ready(1)
-
-        @pl.loop(jnp.where(h == late, 0, jnp.minimum(2 * h - 11, h - 1)), jnp.minimum(2 * h - 9, h))
-        def _(s):
-            send_part(s)
-
-        @pl.loop(jnp.clip(2 * (h - 10), 0, jnp.clip(h - 8, 0, 5)), jnp.where(h == 13, 5, jnp.clip(2 * (h - 9), 0, jnp.maximum(h - 7, 0))))
+        @pl.loop(*steps_at(h, (2, 3, 4, 4, 5, 5, 5, 5)))
         def _(n):
-            own_part(n)
-
-    last_send_part()
-    own_part(chunks - 2)
-    last_own_part()
+            send_pair(n)
+
+        @pl.loop(*steps_at(h, (10, 10, 10, 10, 10, 11, 12, 13)))
+        def _(k):
+            @pl.when(k >= 10)
+            def _():
+                send_part(k)
+
+        @pl.when(jnp.logical_and(h >= 8, h <= 10))
+        def _():
+            tokens_ready(1, h - 8)
+
+        @pl.loop(*steps_at(h, (0, 0, 2, 6, 10, 12, 18, 18)))
+        def _(k):
+            n, m = unit(k)
+            own_product(n, m)
+
+            @pl.when(k < 15)
+            def _():
+                own_finish(n, m)
+
+    @pl.loop(0, PIECES)
+    def _(m):
+        own_finish(chunks - 2, m)
+
+    last_up_ahead()
+    last_up()
+    last_own(0)
+    last_own(1)
 
     @pl.loop(0, 2 * chunks)
     def _(h):
@@ -406,8 +440,8 @@
             outward(r, p, j, i, 1, outer).wait_send()
 
     for m in range(PIECES):
-        kept_sums(m).wait()
         for g in range(2):
+            kept_sums(g, m).wait()
             last_partial(g, m).wait_send()
             landed(last_got.at[g, lines(m)], o_in.at[last + g, m])
 
@@ -471,6 +505,7 @@
             pltpu.VMEM((2 * chunks, rows, LANES), jnp.bfloat16),
             pltpu.VMEM((2 * chunks, rows, LANES), jnp.bfloat16),
             pltpu.VMEM((rows, 2 * LANES), jnp.float32),
+            pltpu.VMEM((rows, LANES), jnp.float32),
             pltpu.VMEM((chunks, rows, LANES), jnp.bfloat16),
             dma((2 * chunks, 6)),
             dma((2 * chunks, 6)),
@@ -483,7 +518,7 @@
             dma((2 * chunks, PIECES)),
             dma((2 * chunks, PIECES)),
             dma((chunks, PIECES)),
-            dma((PIECES,)),
+            dma((2, PIECES)),
         ],
         compiler_params=pltpu.CompilerParams(
             collective_id=0, has_side_effects=True, vmem_limit_bytes=60 * 2**20

time: 140 us -> 140 us (level)
  no operation moved by 1% of the time
where the time goes in v5:
time: 140 us; the launch traced here: 139 us
  Pallas kernels  139 us (99%)
    pallas_call x1, Pallas kernels, on_device(): pl.pallas_call(kernel, out_shape=(jax.ShapeDtypeStruct((rows, units - LAN...  136 us
    pallas_call x1, Pallas kernels, on_device(): pl.pallas_call(closing, out_shape=jax.ShapeDtypeStruct((rows, units), jnp...  3.04 us

profile of v5, /device:TPU:0, one launch (start us, length us, event | category | flops | bytes accessed | tf_op | source)
XLA Modules:
  0.0 139.5 jit_solution(16693300304588655161)
XLA Ops:
  0.0 136.4 %shard_map.37 = (bf16[768,768]{1,0:T(8,128)(2,1)}, f32[768,256]{1,0:T(8,128)}, bf16[2,768,128]{2,1,0:T(8,128)(2,1)}) custom-call(bf16[768,512]{1,0:T(8,128)(2,1)} %tok.1, bf16[1024,896]{1,0:T(8,128)(2,1)} %gate.1, bf16[1024,896]{1,0:T(8,128)(2,1)} %up.1), custom_call_target="tpu_custom_call" | custom-call | flops 22548578304 | bytes 5832704 | tf_op jit(solution)/shard_map/pallas_call | solution.py:493
  136.4 3.0 %shard_map.38 = bf16[768,896]{1,0:T(8,128)(2,1)} custom-call(bf16[768,768]{1,0:T(8,128)(2,1)} %get-tuple-element.8.hidden, f32[768,256]{1,0:T(8,128)} %get-tuple-element.9.last_own, bf16[2,768,128]{2,1,0:T(8,128)(2,1)} %get-tuple-element.10.last_got), custom_call_target="tpu_custom_call" | custom-call | tf_op jit(solution)/shard_map/pallas_call | solution.py:530

commit v6 on v5

--- a/solution.py
+++ b/solution.py
@@ -310,6 +310,39 @@
         lane = pl.ds(pl.multiple_of(n * LANES, LANES), LANES)
         return pltpu.make_async_copy(out.at[n, lines(m)], hidden.at[lines(m), lane], done.at[n, m])
 
+    sent_early = 8
+
+    def weights_sent(h):
+        for copy in first_half(h) + second_half(h) + relayed(h):
+            copy.wait_send()
+
+    def partial_sent(h):
+        @pl.loop(0, PIECES)
+        def _(m):
+            partial(h, m).wait_send()
+
+    def tokens_sent():
+        for p in range(PIECES):
+            @pl.when(source)
+            def _():
+                flip_pass(p).wait_send()
+                flip_send(p).wait_send()
+
+        @pl.when(jnp.logical_not(source))
+        def _():
+            cross_send(PIECES - 1).wait_send()
+
+        @pl.loop(0, steps)
+        def _(i):
+            r, p, j = i // (2 * PIECES), (i // 2) % PIECES, b * 2
+            outward(r, p, j, i, 0, pair).wait_send()
+            to_sibling(r, p, j, i, 0).wait_send()
+            to_sibling(r, p, j, i, 1).wait_send()
+
+            @pl.when(source)
+            def _():
+                outward(r, p, j, i, 1, outer).wait_send()
+
     barrier = pltpu.get_barrier_semaphore()
     neighbours = (right, left, partner, flip, cross, sibling, pair, outer)
     for to in neighbours:
@@ -392,6 +425,18 @@
             def _():
                 own_finish(n, m)
 
+        weights_sent(h - late)
+
+        @pl.when(h == 11)
+        def _():
+            tokens_sent()
+
+        @pl.when(h == last + 1)
+        def _():
+            @pl.loop(0, sent_early)
+            def _(k):
+                partial_sent(k)
+
     @pl.loop(0, PIECES)
     def _(m):
         own_finish(chunks - 2, m)
@@ -401,43 +446,19 @@
     last_own(0)
     last_own(1)
 
-    @pl.loop(0, 2 * chunks)
+    @pl.loop(sent_early, 2 * chunks)
     def _(h):
-        for copy in first_half(h) + second_half(h) + relayed(h):
-            copy.wait_send()
+        weights_sent(h)
 
         @pl.when(h < last)
         def _():
-            @pl.loop(0, PIECES)
-            def _(m):
-                partial(h, m).wait_send()
+            partial_sent(h)
 
     @pl.loop(0, chunks - 1)
     def _(n):
         @pl.loop(0, PIECES)
         def _(m):
             result(n, m).wait()
-
-    for p in range(PIECES):
-        @pl.when(source)
-        def _():
-            flip_pass(p).wait_send()
-            flip_send(p).wait_send()
-
-    @pl.when(jnp.logical_not(source))
-    def _():
-        cross_send(PIECES - 1).wait_send()
-
-    @pl.loop(0, steps)
-    def _(i):
-        r, p, j = i // (2 * PIECES), (i // 2) % PIECES, b * 2
-        outward(r, p, j, i, 0, pair).wait_send()
-        to_sibling(r, p, j, i, 0).wait_send()
-        to_sibling(r, p, j, i, 1).wait_send()
-
-        @pl.when(source)
-        def _():
-            outward(r, p, j, i, 1, outer).wait_send()
 
     for m in range(PIECES):
         for g in range(2):
@@ -459,15 +480,20 @@
             pltpu.make_async_copy(last_own.at[lines(m)], own.at[lines(m)], sem_in.at[m, 0]),
             pltpu.make_async_copy(last_got.at[0, lines(m)], got.at[0, lines(m)], sem_in.at[m, 1]),
             pltpu.make_async_copy(last_got.at[1, lines(m)], got.at[1, lines(m)], sem_in.at[m, 2]),
-            pltpu.make_async_copy(hidden.at[lines(m)], whole.at[lines(m), pl.ds(0, known)], sem_in.at[m, 3]),
         )
 
-    def store(m):
-        return pltpu.make_async_copy(whole.at[lines(m)], out.at[lines(m)], sem_out.at[m])
+    def load_known(m):
+        return pltpu.make_async_copy(hidden.at[lines(m)], whole.at[lines(m), pl.ds(0, known)], sem_in.at[m, 3])
+
+    def store(m, i):
+        lane = pl.ds(known, LANES) if i else pl.ds(0, known)
+        return pltpu.make_async_copy(whole.at[lines(m), lane], out.at[lines(m), lane], sem_out.at[m, i])
 
     for m in range(PIECES):
         for copy in loads(m):
             copy.start()
+    for m in range(PIECES):
+        load_known(m).start()
     for m in range(PIECES):
         for copy in loads(m):
             copy.wait()
@@ -479,9 +505,12 @@
             u = own[here, LANES:] + decode(got[1, here, :])
             whole[here, pl.ds(known, LANES)] = (g / (1.0 + jnp.exp(-g)) * u).astype(out.dtype)
 
-        store(m).start()
+        store(m, 1).start()
+        load_known(m).wait()
+        store(m, 0).start()
     for m in range(PIECES):
-        store(m).wait()
+        for i in range(2):
+            store(m, i).wait()
 
 
 def on_device(tokens, gate_weight, up_weight):
@@ -537,7 +566,7 @@
             pltpu.VMEM((rows, 2 * LANES), jnp.float32),
             pltpu.VMEM((2, rows, LANES), jnp.bfloat16),
             dma((PIECES, 4)),
-            dma((PIECES,)),
+            dma((PIECES, 2)),
         ],
     )(*parts)
 

time: 140 us -> 140 us (level)
  no operation moved by 1% of the time
where the time goes in v6:
time: 140 us
  Pallas kernels  140 us (100%)
    pallas_call x1, Pallas kernels, on_device(): pl.pallas_call(kernel, out_shape=(jax.ShapeDtypeStruct((rows, units - LAN...  137 us
    pallas_call x1, Pallas kernels, on_device(): pl.pallas_call(closing, out_shape=jax.ShapeDtypeStruct((rows, units), jnp...  2.97 us

profile of v6, /device:TPU:0, one launch (start us, length us, event | category | flops | bytes accessed | tf_op | source)
XLA Modules:
  0.0 139.6 jit_solution(3254186373127021317)
XLA Ops:
  0.0 136.6 %shard_map.37 = (bf16[768,768]{1,0:T(8,128)(2,1)}, f32[768,256]{1,0:T(8,128)}, bf16[2,768,128]{2,1,0:T(8,128)(2,1)}) custom-call(bf16[768,512]{1,0:T(8,128)(2,1)} %tok.1, bf16[1024,896]{1,0:T(8,128)(2,1)} %gate.1, bf16[1024,896]{1,0:T(8,128)(2,1)} %up.1), custom_call_target="tpu_custom_call" | custom-call | flops 22548578304 | bytes 5832704 | tf_op jit(solution)/shard_map/pallas_call | solution.py:522
  136.6 3.0 %shard_map.38 = bf16[768,896]{1,0:T(8,128)(2,1)} custom-call(bf16[768,768]{1,0:T(8,128)(2,1)} %get-tuple-element.8.hidden, f32[768,256]{1,0:T(8,128)} %get-tuple-element.9.last_own, bf16[2,768,128]{2,1,0:T(8,128)(2,1)} %get-tuple-element.10.last_got), custom_call_target="tpu_custom_call" | custom-call | tf_op jit(solution)/shard_map/pallas_call | solution.py:559

commit v7 on v5

--- a/solution.py
+++ b/solution.py
@@ -156,8 +156,6 @@
     def cross_step(p):
         @pl.when(jnp.logical_not(source))
         def _():
-            if p:
-                cross_send(p - 1).wait_send()
             cross_send(p).start()
 
     def flip_step(p):
@@ -321,7 +319,8 @@
 
     start_first(0)
     start_second(0)
-    cross_step(0)
+    for p in range(PIECES):
+        cross_step(p)
 
     @pl.when(source)
     def _():
@@ -331,7 +330,7 @@
     start_first(1)
 
     early = (
-        ((cross_step, 1), (near_step, 0, 0, 0), (cross_step, 2), (near_step, 0, 1, 0)),
+        ((near_step, 0, 0, 0), (near_step, 0, 1, 0)),
         ((near_step, 0, 0, 1), (far_step, 0, 0, 0), (near_step, 0, 2, 0), (near_step, 0, 1, 1), (far_step, 0, 1, 0), (last_step, 0, 0, 0)),
         ((near_step, 0, 2, 1), (far_step, 0, 0, 1), (last_step, 0, 1, 0), (flip_step, 0)),
         ((near_step, *own_rows(0)), (far_step, 0, 2, 0), (last_step, 0, 0, 1), (flip_step, 1), (far_step, 0, 1, 1), (last_step, 0, 2, 0), (flip_step, 2)),
@@ -426,7 +425,8 @@
 
     @pl.when(jnp.logical_not(source))
     def _():
-        cross_send(PIECES - 1).wait_send()
+        for p in range(PIECES):
+            cross_send(p).wait_send()
 
     @pl.loop(0, steps)
     def _(i):

time: 140 us -> 140 us (level)
  no operation moved by 1% of the time
where the time goes in v7:
time: 140 us; the launch traced here: 139 us
  Pallas kernels  139 us (99%)
    pallas_call x1, Pallas kernels, on_device(): pl.pallas_call(kernel, out_shape=(jax.ShapeDtypeStruct((rows, units - LAN...  136 us
    pallas_call x1, Pallas kernels, on_device(): pl.pallas_call(closing, out_shape=jax.ShapeDtypeStruct((rows, units), jnp...  3.04 us

profile of v7, /device:TPU:0, one launch (start us, length us, event | category | flops | bytes accessed | tf_op | source)
XLA Modules:
  0.0 139.5 jit_solution(18130271616659648135)
XLA Ops:
  0.0 136.4 %shard_map.37 = (bf16[768,768]{1,0:T(8,128)(2,1)}, f32[768,256]{1,0:T(8,128)}, bf16[2,768,128]{2,1,0:T(8,128)(2,1)}) custom-call(bf16[768,512]{1,0:T(8,128)(2,1)} %tok.1, bf16[1024,896]{1,0:T(8,128)(2,1)} %gate.1, bf16[1024,896]{1,0:T(8,128)(2,1)} %up.1), custom_call_target="tpu_custom_call" | custom-call | flops 22548578304 | bytes 5832704 | tf_op jit(solution)/shard_map/pallas_call | solution.py:493
  136.4 3.0 %shard_map.38 = bf16[768,896]{1,0:T(8,128)(2,1)} custom-call(bf16[768,768]{1,0:T(8,128)(2,1)} %get-tuple-element.8.hidden, f32[768,256]{1,0:T(8,128)} %get-tuple-element.9.last_own, bf16[2,768,128]{2,1,0:T(8,128)(2,1)} %get-tuple-element.10.last_got), custom_call_target="tpu_custom_call" | custom-call | tf_op jit(solution)/shard_map/pallas_call | solution.py:530
